TPU v7x, 32 devices: a whole 2x2x4 slice. The times are simulated.
32 devices in a mesh: rep: 4 (over y, x), shard: 8 (over z, core).
Axes of the slice: x: 2, y: 2, z: 4, core: 2. Of those that a mesh axis runs over, the one named last changes fastest.
Arguments:
- local_dense: float32 [4, 1024, 1024], P('rep', 'shard'), may hold values from -6 to 6
- anchor_dense: float32 [1024, 1024], P('shard'), may hold values from -6 to 6
- momentum_dense: float32 [1024, 1024], P('shard'), may hold values from -6 to 6
- local_emb: float32 [4, 8192, 2048], P('rep', 'shard'), may hold values from -24 to 24
- anchor_emb: float32 [8192, 2048], P('shard'), may hold values from -24 to 24
- momentum_emb: float32 [8192, 2048], P('shard'), may hold values from -6 to 6
- proj_basis: float32 [2048, 64], P('shard'), may hold values from -6 to 6
Outputs:
- new_dense_anchor: float32 [1024, 1024], P('shard')
- new_dense_momentum: float32 [1024, 1024], P('shard')
- dense_weights: bfloat16 [1024, 1024], replicated
- new_emb_anchor: float32 [8192, 2048], P('shard')
- new_emb_momentum: float32 [8192, 2048], P('shard')
All inputs are finite; a program needn't handle non-finite values.
Results may differ from a plain program's by a relative error of at most 0.0004.
Values may be sent and summed in bfloat16 or wider, within the bound.
A program may use at most 128 MiB of HBM per device.

v0:
```python
import jax
import jax.numpy as jnp
from jax import lax
from jax.sharding import PartitionSpec as P

outer_rate = 0.7
momentum_rate = 0.9
highest = lax.Precision.HIGHEST


def dense_update(dense_sum, anchor_dense, momentum_dense, group_count):
    dense_grad = dense_sum / group_count
    dense_mom = momentum_rate * momentum_dense + dense_grad
    dense_new = anchor_dense - outer_rate * (dense_grad + momentum_rate * dense_mom)
    gathered = lax.all_gather(dense_new.astype(jnp.bfloat16), "shard", axis=0, tiled=True)
    return (dense_new, dense_mom, gathered)


def on_device(
    local_dense, anchor_dense, momentum_dense, local_emb, anchor_emb, momentum_emb, proj_basis
):
    group_count = lax.axis_size("rep")
    full_basis = lax.all_gather(proj_basis, "shard", axis=0, tiled=True)
    dense_diff = anchor_dense - local_dense[0]
    emb_diff = anchor_emb - local_emb[0]
    part_factor = jnp.dot(
        emb_diff, full_basis, precision=highest, preferred_element_type=jnp.float32
    )
    dense_sum, factor = lax.psum((dense_diff, part_factor), "rep")
    dense_new, dense_mom, gathered = dense_update(
        dense_sum, anchor_dense, momentum_dense, group_count
    )
    local_gram = lax.dot_general(
        factor,
        factor,
        (((0,), (0,)), ((), ())),
        precision=highest,
        preferred_element_type=jnp.float32,
    )
    gram_matrix = lax.psum(local_gram, "shard")
    chol_lower = jnp.linalg.cholesky(gram_matrix)
    ortho_rows = jax.scipy.linalg.solve_triangular(chol_lower, factor.T, lower=True).T
    coeff_share = lax.psum_scatter(
        lax.dot_general(
            emb_diff,
            ortho_rows,
            (((0,), (0,)), ((), ())),
            precision=highest,
            preferred_element_type=jnp.float32,
        ),
        "shard",
        scatter_dimension=0,
        tiled=True,
    )
    coeff_share = lax.psum(coeff_share, "rep")
    coefficients = lax.all_gather(coeff_share, "shard", axis=0, tiled=True)
    emb_grad = (
        lax.dot_general(
            ortho_rows,
            coefficients,
            (((1,), (1,)), ((), ())),
            precision=highest,
            preferred_element_type=jnp.float32,
        )
        / group_count
    )
    emb_mom = momentum_rate * momentum_emb + emb_grad
    emb_new = anchor_emb - outer_rate * (emb_grad + momentum_rate * emb_mom)
    return (dense_new, dense_mom, gathered, emb_new, emb_mom)


def solution(mesh):
    placed = (
        P("rep", "shard", None),
        P("shard", None),
        P("shard", None),
        P("rep", "shard", None),
        P("shard", None),
        P("shard", None),
        P("shard", None),
    )
    return jax.shard_map(
        on_device,
        mesh=mesh,
        in_specs=placed,
        out_specs=(P("shard", None), P("shard", None), P(), P("shard", None), P("shard", None)),
        check_vma=False,
    )
```

profile of v0, /device:TPU:0, one launch (start us, length us, event | category | flops | bytes accessed | tf_op | source)
XLA Modules:
  0.0 270.5 jit_solution(2345077583079396937)
XLA Ops:
  7.2 0.0 all-reduce.4.cloned.1.call-start
  7.2 16.8 %all_gather.10 = f32[2048,64]{0,1:T(8,128)S(1)} all-gather(f32[256,64]{0,1:T(8,128)} %param.13), channel_id=1, replica_groups=mesh['rep'=4,'shard'=8] {'shard'}, dimensions={0}, use_global_device_ids=true | all-gather | bytes 589824 | tf_op jit(solution)/shard_map/all_gather | solution.py:23
  24.0 12.6 %fusion.1 = f32[1024,64]{0,1:T(8,128)} fusion(f32[2048,64]{0,1:T(8,128)S(1)} %all_gather.10, f32[1024,2048]{1,0:T(8,128)} %param.11, f32[1,1024,2048]{2,1,0:T(8,128)} %param.10), kind=kOutput, calls=%fused_computation.4 | convolution fusion | flops 1612709888 | bytes 17563648 | tf_op jit(solution)/shard_map/dot_general | solution.py:26
  36.6 0.0 all-reduce.4.cloned.1.call-update
  36.6 0.0 reduce-scatter.2.cloned.1.call-start
  36.7 44.1 %all-reduce.4.cloned.1.call-done = f32[1024,64]{0,1:T(8,128)} async-done(((f32[1024,64]{0,1:T(8,128)}), f32[1024,64]{0,1:T(8,128)}) %all-reduce.4.cloned.1.call-update) | async-done | bytes 262160 | tf_op jit(solution)/shard_map/psum | solution.py:29
  80.8 1.4 fusion.7
  82.2 28.2 %psum.30 = f32[64,64]{0,1:T(8,128)S(1)} all-reduce(f32[64,64]{0,1:T(8,128)S(1)} %fusion.7), channel_id=1, replica_groups=mesh['rep'=4,'shard'=8] {'shard'}, use_global_device_ids=true, to_apply=%region_2.0 | all-reduce | flops 4096 | bytes 32768 | tf_op jit(solution)/shard_map/psum | solution.py:40
  110.3 0.1 copy.13
  110.4 5.8 %cholesky.16 = f32[64,64]{1,0:T(8,128)S(1)} custom-call(f32[64,64]{1,0:T(8,128)S(1)} %fusion.5), custom_call_target="Cholesky" | custom-call | tf_op jit(solution)/shard_map/jit(cholesky)/cholesky | solution.py:41
  116.3 0.6 compare_reduce_fusion
  116.9 0.7 fusion.2
  117.6 4.9 %custom-call.7 = f32[1,64,64]{1,2,0:T(8,128)S(1)} custom-call(f32[1,64,64]{2,1,0:T(8,128)S(1)} %fusion.2), custom_call_target="InvertDiagBlocksLowerTriangular" | custom-call | tf_op jit(solution)/shard_map/jit(_solve_triangular)/triangular_solve | solution.py:42
  122.5 1.4 fusion.3
  123.9 0.0 copy-start
  123.9 0.0 copy-start.1
  123.9 0.0 copy-start.2
  123.9 17.9 %fusion = f32[2048,64]{1,0:T(8,128)} fusion(f32[64,1024]{1,0:T(8,128)S(1)} %fusion.3, f32[1024,2048]{1,0:T(8,128)} %param.11, f32[1,1024,2048]{2,1,0:T(8,128)} %param.10), kind=kOutput, calls=%fused_computation.3 | convolution fusion | flops 1612709888 | bytes 17563648 | tf_op jit(solution)/shard_map/dot_general | solution.py:44
  141.9 0.0 reduce-scatter.2.cloned.1.call-update
  141.9 0.0 all-reduce.6.cloned.1.call-start
  141.9 0.0 copy-done
  141.9 0.0 copy-done.1
  142.0 0.9 bitcast_subtract_fusion.3
  142.8 28.8 %reduce-scatter.2.cloned.1.call-done = f32[256,64]{1,0:T(8,128)} async-done(((f32[2048,64]{1,0:T(8,128)}), f32[256,64]{1,0:T(8,128)}) %reduce-scatter.2.cloned.1.call-update) | async-done | bytes 65552 | tf_op jit(solution)/shard_map/reduce_scatter | solution.py:43
  171.6 0.0 all-reduce.6.cloned.1.call-update
  171.6 0.0 all-gather.2.cloned.1.call-start
  171.6 49.2 %all-reduce.6.cloned.1.call-done = (f32[128,1024]{1,0:T(8,128)}, f32[256,64]{1,0:T(8,128)}) async-done(((f32[128,1024]{1,0:T(8,128)}, f32[256,64]{1,0:T(8,128)}), (f32[128,1024]{1,0:T(8,128)}, f32[256,64]{1,0:T(8,128)})) %all-reduce.6.cloned.1.call-update) | async-done | bytes 589840 | tf_op jit(solution)/shard_map/psum | solution.py:29
  220.9 0.0 copy-done.2
  220.9 2.3 fusion.6
  223.1 0.0 all-gather.2.cloned.1.call-update
  223.1 22.0 %all_gather.11 = f32[2048,64]{1,0:T(8,128)S(1)} all-gather(f32[256,64]{1,0:T(8,128)} %get-tuple-element.6), channel_id=1, replica_groups=mesh['rep'=4,'shard'=8] {'shard'}, dimensions={0}, use_global_device_ids=true | all-gather | bytes 589824 | tf_op jit(solution)/shard_map/all_gather | solution.py:56
  245.2 15.7 %multiply_subtract_fusion = (f32[1024,2048]{1,0:T(8,128)}, f32[1024,2048]{1,0:T(8,128)}) fusion(f32[1024,2048]{1,0:T(8,128)} %param.11, f32[1024,2048]{1,0:T(8,128)} %param.12, f32[64,1024]{1,0:T(8,128)S(1)} %fusion.3, f32[2048,64]{1,0:T(8,128)S(1)} %all_gather.11), kind=kOutput, calls=%fused_computation.1 | convolution fusion | flops 1625292800 | bytes 34340864 | tf_op jit(solution)/shard_map/dot_general | solution.py:58
  260.9 0.0 all-gather.2.cloned.1.call-done
  260.9 3.1 %copy.19 = bf16[1024,1024]{1,0:T(8,128)(2,1)} copy(bf16[1024,1024]{1,0:T(8,128)(2,1)} %all-gather.2.cloned.1.call-done) | data formatting | bytes 4194304
  (2 shorter events, 0.0 us)
Async XLA Ops:
  7.2 73.6 %all-reduce.4.cloned.1.call-start = ((), (), s32[]{:S(2)}) async-start(), calls=%async_computation.2 | async-start | bytes 524288 | tf_op jit(solution)/shard_map/psum | solution.py:29
  36.6 134.9 %reduce-scatter.2.cloned.1.call-start = ((), (), s32[]{:S(2)}) async-start(), calls=%async_computation.3 | async-start | bytes 1179648 | tf_op jit(solution)/shard_map/reduce_scatter | solution.py:43
  123.9 18.1 %copy-start = (f32[128,1024]{1,0:T(8,128)S(1)}, f32[128,1024]{1,0:T(8,128)}, u32[]{:S(2)}) copy-start(f32[128,1024]{1,0:T(8,128)} %param.8) | copy-start | bytes 1572868
  123.9 18.1 %copy-start.1 = (f32[1,128,1024]{2,1,0:T(8,128)S(1)}, f32[1,128,1024]{2,1,0:T(8,128)}, u32[]{:S(2)}) copy-start(f32[1,128,1024]{2,1,0:T(8,128)} %param.7) | copy-start | bytes 1572868
  123.9 97.0 %copy-start.2 = (f32[128,1024]{1,0:T(8,128)S(1)}, f32[128,1024]{1,0:T(8,128)}, u32[]{:S(2)}) copy-start(f32[128,1024]{1,0:T(8,128)} %param.9) | copy-start | bytes 1572868
  141.9 79.0 %all-reduce.6.cloned.1.call-start = ((), (), s32[]{:S(2)}) async-start(), calls=%async_computation.4 | async-start | bytes 1310720 | tf_op jit(solution)/shard_map/psum | solution.py:29
  171.6 89.3 %all-gather.2.cloned.1.call-start = ((), (), s32[]{:S(2)}) async-start(), calls=%async_computation.1 | async-start | bytes 2359296 | tf_op jit(solution)/shard_map/all_gather | solution.py:15
Sparse Core Ops, SparseCore 0:
  36.7 43.9 all-reduce.3
  142.0 29.5 reduce-scatter.1
  175.5 45.3 all-reduce.5
  223.3 33.0 all-gather.1
where the time goes:
time: 271 us; the launch traced here: 270 us
  waiting for transfers between devices  122 us (45%)
  blocking collectives  67 us (25%)
  matrix products  49 us (18%)
  other arithmetic  15.2 us (6%)
  between operations  13.8 us (5%)
  local copies, waits for them, and re-layouts  3.17 us (1%)
    psum x2, waiting for transfers between devices, on_device(): dense_sum, factor = lax.psum((dense_diff, part_factor), 'rep')  93.3 us
    reduce_scatter x1, waiting for transfers between devices, on_device(): lax.psum_scatter(lax.dot_general(emb_diff, ortho_rows, (((0,), (0,)), (()...  28.8 us
    psum x1, blocking collectives, on_device(): gram_matrix = lax.psum(local_gram, 'shard')  28.2 us
    all_gather x1, blocking collectives, on_device(): coefficients = lax.all_gather(coeff_share, 'shard', axis=0, tiled=True)  22 us
    dot_general x1, matrix products, on_device(): lax.dot_general(emb_diff, ortho_rows, (((0,), (0,)), ((), ())), precision...  17.9 us
    all_gather x1, blocking collectives, on_device(): full_basis = lax.all_gather(proj_basis, 'shard', axis=0, tiled=True)  16.8 us
    dot_general x1, matrix products, on_device(): lax.dot_general(ortho_rows, coefficients, (((1,), (1,)), ((), ())), preci...  15.7 us
    dot_general x1, matrix products, on_device(): jnp.dot(emb_diff, full_basis, precision=highest, preferred_element_type=j...  12.6 us
  transfers between devices with their start and end apart: 4, of which 3 were waited for; matrix products, arithmetic and copies ran while one was open for 6% of the time, Pallas kernels for 0%

commit v1 on v0

--- a/solution.py
+++ b/solution.py
@@ -1,3 +1,4 @@
+import functools
 import jax
 import jax.numpy as jnp
 from jax import lax
@@ -6,6 +7,14 @@
 outer_rate = 0.7
 momentum_rate = 0.9
 highest = lax.Precision.HIGHEST
+
+
+def see_point(a0, lane_axis):
+    taken_in = jnp.sum(lax.all_gather(a0, axis_name=lane_axis), axis=0)
+    return taken_in
+
+
+follow_tables = functools.partial(see_point, lane_axis="shard")
 
 
 def dense_update(dense_sum, anchor_dense, momentum_dense, group_count):
@@ -37,7 +46,7 @@
         precision=highest,
         preferred_element_type=jnp.float32,
     )
-    gram_matrix = lax.psum(local_gram, "shard")
+    gram_matrix = follow_tables(local_gram)
     chol_lower = jnp.linalg.cholesky(gram_matrix)
     ortho_rows = jax.scipy.linalg.solve_triangular(chol_lower, factor.T, lower=True).T
     coeff_share = lax.psum_scatter(

time: 271 us -> 260 us (0.959)
  blocking collectives: 67 us -> 53.3 us
  waiting for transfers between devices: 122 us -> 125 us
    psum x1 -> x0, blocking collectives: 28.2 us -> none  [on_device(): gram_matrix = lax.psum(local_gram, 'shard')]
    all_gather x0 -> x1, blocking collectives: none -> 14.4 us  [see_point(): taken_in = jnp.sum(lax.all_gather(a0, axis_name=lane_axis), axis=0)]
    reduce_scatter x1, waiting for transfers between devices: 28.8 us -> 31.6 us  [on_device(): lax.psum_scatter(lax.dot_general(emb_diff, ortho_rows, (((0,), (0,)), (()...]
where the time goes in v1:
time: 260 us
  waiting for transfers between devices  125 us (48%)
  blocking collectives  53.3 us (20%)
  matrix products  49 us (19%)
  other arithmetic  15.2 us (6%)
  between operations  13.8 us (5%)
  local copies, waits for them, and re-layouts  3.17 us (1%)
    psum x2, waiting for transfers between devices, on_device(): dense_sum, factor = lax.psum((dense_diff, part_factor), 'rep')  93.3 us
    reduce_scatter x1, waiting for transfers between devices, on_device(): lax.psum_scatter(lax.dot_general(emb_diff, ortho_rows, (((0,), (0,)), (()...  31.6 us
    all_gather x1, blocking collectives, on_device(): coefficients = lax.all_gather(coeff_share, 'shard', axis=0, tiled=True)  22 us
    dot_general x1, matrix products, on_device(): lax.dot_general(emb_diff, ortho_rows, (((0,), (0,)), ((), ())), precision...  17.9 us
    all_gather x1, blocking collectives, on_device(): full_basis = lax.all_gather(proj_basis, 'shard', axis=0, tiled=True)  16.8 us
    dot_general x1, matrix products, on_device(): lax.dot_general(ortho_rows, coefficients, (((1,), (1,)), ((), ())), preci...  15.7 us
    all_gather x1, blocking collectives, see_point(): taken_in = jnp.sum(lax.all_gather(a0, axis_name=lane_axis), axis=0)  14.4 us
    dot_general x1, matrix products, on_device(): jnp.dot(emb_diff, full_basis, precision=highest, preferred_element_type=j...  12.6 us
  transfers between devices with their start and end apart: 4, of which 3 were waited for; matrix products, arithmetic and copies ran while one was open for 6% of the time, Pallas kernels for 0%

profile of v1, /device:TPU:0, one launch (start us, length us, event | category | flops | bytes accessed | tf_op | source)
XLA Modules:
  0.0 259.6 jit_solution(11226497604541571713)
XLA Ops:
  7.2 0.0 all-reduce.4.cloned.1.call-start
  7.2 16.8 %all_gather.16 = f32[2048,64]{0,1:T(8,128)S(1)} all-gather(f32[256,64]{0,1:T(8,128)} %param.13), channel_id=1, replica_groups=mesh['rep'=4,'shard'=8] {'shard'}, dimensions={0}, use_global_device_ids=true | all-gather | bytes 589824 | tf_op jit(solution)/shard_map/all_gather | solution.py:32
  24.0 12.6 %fusion.1 = f32[1024,64]{0,1:T(8,128)} fusion(f32[2048,64]{0,1:T(8,128)S(1)} %all_gather.16, f32[1024,2048]{1,0:T(8,128)} %param.11, f32[1,1024,2048]{2,1,0:T(8,128)} %param.10), kind=kOutput, calls=%fused_computation.4 | convolution fusion | flops 1612709888 | bytes 17563648 | tf_op jit(solution)/shard_map/dot_general | solution.py:35
  36.6 0.0 all-reduce.4.cloned.1.call-update
  36.6 0.0 reduce-scatter.2.cloned.1.call-start
  36.7 44.1 %all-reduce.4.cloned.1.call-done = f32[1024,64]{0,1:T(8,128)} async-done(((f32[1024,64]{0,1:T(8,128)}), f32[1024,64]{0,1:T(8,128)}) %all-reduce.4.cloned.1.call-update) | async-done | bytes 262160 | tf_op jit(solution)/shard_map/psum | solution.py:38
  80.8 1.4 fusion.7
  82.2 14.4 %all-gather = f32[512,64]{1,0:T(8,128)S(1)} all-gather(f32[64,64]{1,0:T(8,128)S(1)} %fusion.7), channel_id=2, replica_groups=mesh['rep'=4,'shard'=8] {'shard'}, dimensions={0}, use_global_device_ids=true | all-gather | bytes 147456 | tf_op jit(solution)/shard_map/all_gather | solution.py:13
  96.6 0.1 copy.13
  96.7 5.8 %cholesky.16 = f32[64,64]{1,0:T(8,128)S(1)} custom-call(f32[64,64]{1,0:T(8,128)S(1)} %fusion.5), custom_call_target="Cholesky" | custom-call | tf_op jit(solution)/shard_map/jit(cholesky)/cholesky | solution.py:50
  102.6 0.6 compare_reduce_fusion
  103.2 0.7 fusion.2
  103.9 4.9 %custom-call.7 = f32[1,64,64]{1,2,0:T(8,128)S(1)} custom-call(f32[1,64,64]{2,1,0:T(8,128)S(1)} %fusion.2), custom_call_target="InvertDiagBlocksLowerTriangular" | custom-call | tf_op jit(solution)/shard_map/jit(_solve_triangular)/triangular_solve | solution.py:51
  108.8 1.4 fusion.3
  110.2 0.0 copy-start
  110.2 0.0 copy-start.1
  110.2 0.0 copy-start.2
  110.2 17.9 %fusion = f32[2048,64]{1,0:T(8,128)} fusion(f32[64,1024]{1,0:T(8,128)S(1)} %fusion.3, f32[1024,2048]{1,0:T(8,128)} %param.11, f32[1,1024,2048]{2,1,0:T(8,128)} %param.10), kind=kOutput, calls=%fused_computation.3 | convolution fusion | flops 1612709888 | bytes 17563648 | tf_op jit(solution)/shard_map/dot_general | solution.py:53
  128.2 0.0 reduce-scatter.2.cloned.1.call-update
  128.2 0.0 all-reduce.6.cloned.1.call-start
  128.2 0.0 copy-done
  128.2 0.0 copy-done.1
  128.3 0.9 bitcast_subtract_fusion.3
  129.1 31.6 %reduce-scatter.2.cloned.1.call-done = f32[256,64]{1,0:T(8,128)} async-done(((f32[2048,64]{1,0:T(8,128)}), f32[256,64]{1,0:T(8,128)}) %reduce-scatter.2.cloned.1.call-update) | async-done | bytes 65552 | tf_op jit(solution)/shard_map/reduce_scatter | solution.py:52
  160.7 0.0 all-reduce.6.cloned.1.call-update
  160.7 0.0 all-gather.3.cloned.1.call-start
  160.8 49.2 %all-reduce.6.cloned.1.call-done = (f32[128,1024]{1,0:T(8,128)}, f32[256,64]{1,0:T(8,128)}) async-done(((f32[128,1024]{1,0:T(8,128)}, f32[256,64]{1,0:T(8,128)}), (f32[128,1024]{1,0:T(8,128)}, f32[256,64]{1,0:T(8,128)})) %all-reduce.6.cloned.1.call-update) | async-done | bytes 589840 | tf_op jit(solution)/shard_map/psum | solution.py:38
  210.0 0.0 copy-done.2
  210.0 2.3 fusion.6
  212.2 0.0 all-gather.3.cloned.1.call-update
  212.3 22.0 %all_gather.19 = f32[2048,64]{1,0:T(8,128)S(1)} all-gather(f32[256,64]{1,0:T(8,128)} %get-tuple-element.6), channel_id=1, replica_groups=mesh['rep'=4,'shard'=8] {'shard'}, dimensions={0}, use_global_device_ids=true | all-gather | bytes 589824 | tf_op jit(solution)/shard_map/all_gather | solution.py:65
  234.3 15.7 %multiply_subtract_fusion = (f32[1024,2048]{1,0:T(8,128)}, f32[1024,2048]{1,0:T(8,128)}) fusion(f32[1024,2048]{1,0:T(8,128)} %param.11, f32[1024,2048]{1,0:T(8,128)} %param.12, f32[64,1024]{1,0:T(8,128)S(1)} %fusion.3, f32[2048,64]{1,0:T(8,128)S(1)} %all_gather.19), kind=kOutput, calls=%fused_computation.1 | convolution fusion | flops 1625292800 | bytes 34340864 | tf_op jit(solution)/shard_map/dot_general | solution.py:67
  250.0 0.0 all-gather.3.cloned.1.call-done
  250.0 3.1 %copy.18 = bf16[1024,1024]{1,0:T(8,128)(2,1)} copy(bf16[1024,1024]{1,0:T(8,128)(2,1)} %all-gather.3.cloned.1.call-done) | data formatting | bytes 4194304
  (3 shorter events, 0.1 us)
Async XLA Ops:
  7.2 73.6 %all-reduce.4.cloned.1.call-start = ((), (), s32[]{:S(2)}) async-start(), calls=%async_computation.2 | async-start | bytes 524288 | tf_op jit(solution)/shard_map/psum | solution.py:38
  36.6 124.1 %reduce-scatter.2.cloned.1.call-start = ((), (), s32[]{:S(2)}) async-start(), calls=%async_computation.3 | async-start | bytes 1179648 | tf_op jit(solution)/shard_map/reduce_scatter | solution.py:52
  110.2 18.1 %copy-start = (f32[128,1024]{1,0:T(8,128)S(1)}, f32[128,1024]{1,0:T(8,128)}, u32[]{:S(2)}) copy-start(f32[128,1024]{1,0:T(8,128)} %param.8) | copy-start | bytes 1572868
  110.2 18.1 %copy-start.1 = (f32[1,128,1024]{2,1,0:T(8,128)S(1)}, f32[1,128,1024]{2,1,0:T(8,128)}, u32[]{:S(2)}) copy-start(f32[1,128,1024]{2,1,0:T(8,128)} %param.7) | copy-start | bytes 1572868
  110.2 99.8 %copy-start.2 = (f32[128,1024]{1,0:T(8,128)S(1)}, f32[128,1024]{1,0:T(8,128)}, u32[]{:S(2)}) copy-start(f32[128,1024]{1,0:T(8,128)} %param.9) | copy-start | bytes 1572868
  128.2 81.8 %all-reduce.6.cloned.1.call-start = ((), (), s32[]{:S(2)}) async-start(), calls=%async_computation.4 | async-start | bytes 1310720 | tf_op jit(solution)/shard_map/psum | solution.py:38
  160.7 89.3 %all-gather.3.cloned.1.call-start = ((), (), s32[]{:S(2)}) async-start(), calls=%async_computation.1 | async-start | bytes 2359296 | tf_op jit(solution)/shard_map/all_gather | solution.py:24
Sparse Core Ops, SparseCore 0:
  36.7 43.9 all-reduce.3
  128.3 32.3 reduce-scatter.1
  164.6 45.3 all-reduce.5
  212.4 33.0 all-gather.2
